TPU v7x, 512 devices: a whole 4x8x8 slice. The times are simulated.
512 devices in a mesh: dp: 8 (over x, core), worker: 64 (over z, y).
Axes of the slice: x: 4, y: 8, z: 8, core: 2. Of those that a mesh axis runs over, the one named last changes fastest.
Arguments:
- partials: bfloat16 [8, 192, 512, 512], P('dp', None, 'worker'), may hold values from -6 to 6
- stats: float32 [8, 64, 2, 512, 512], P('dp', 'worker'), as said below
- roots: bfloat16 [8, 64, 2, 512, 512], P('dp', 'worker'), as said below
- owner: int32 [192], replicated, may hold values from 0 to 63, as said below
- refresh: int32 [64], replicated, may hold values from 0 to 191, as said below
Outputs:
- directions: bfloat16 [192, 512, 512], P('dp', 'worker')
Inputs may be any that keep to these rules, and one draw needn't show every extreme that they name: `owner`: within the 24 blocks of one group, blocks r * 24 to r * 24 + 23, the owners are distinct workers. `refresh`: 64 distinct block indices. `stats`: each matrix is symmetric positive definite. `roots`: each matrix is symmetric positive definite.
All inputs are finite; a program needn't handle non-finite values.
Results may differ from a plain program's by a relative error of at most 0.02.
Values may be sent and summed in bfloat16 or wider, within the bound.
A program may use at most 64 MiB of HBM per device.

v0:
```python
import jax
import jax.numpy as jnp
from jax import lax
from jax.sharding import PartitionSpec as P

ITERS = 3


STAT_DECAY = 0.9
EPSILON = 1e-06


def matmul(left_operand, right_operand):
    return jnp.dot(left_operand, right_operand, preferred_element_type=jnp.float32)


def normalize(stat_matrix):
    frob_scale = jnp.sqrt(jnp.sum(stat_matrix * stat_matrix) + EPSILON)
    return (stat_matrix / frob_scale).astype(jnp.bfloat16)


def newton(current):
    block_order = current.shape[0]
    identity = jnp.eye(block_order, dtype=jnp.float32)
    root_iter = current
    for iteration in range(ITERS):
        factor = ((5.0 * identity - current.astype(jnp.float32)) * 0.25).astype(jnp.bfloat16)
        if iteration == 0:
            root_iter = factor
        else:
            root_iter = matmul(root_iter, factor).astype(jnp.bfloat16)
        if iteration + 1 < ITERS:
            square = matmul(factor, factor).astype(jnp.bfloat16)
            partial_prod = matmul(square, current).astype(jnp.bfloat16)
            current = matmul(partial_prod, square).astype(jnp.bfloat16)
    return root_iter


def slot_flags(owner, refresh, group_row, worker_index, blocks_row):
    first_block = group_row * blocks_row
    owners_row = lax.dynamic_slice_in_dim(owner, first_block, blocks_row)
    block_ids = first_block + jnp.arange(blocks_row, dtype=jnp.int32)
    listed = jnp.sum((block_ids[:, None] == refresh[None, :]).astype(jnp.int32), axis=1) > 0
    fresh_flag = jnp.any((owners_row == worker_index) & listed)
    return (owners_row, fresh_flag, listed)


def on_device(partials, stats, roots, owner, refresh):
    workers = lax.axis_size("worker")
    replicas = lax.axis_size("dp")
    row_slice = partials.shape[2]
    block_order = partials.shape[3]
    blocks_row = partials.shape[1] // replicas
    row_index = lax.axis_index("dp")
    worker_index = lax.axis_index("worker")
    worker_ids = jnp.arange(workers, dtype=jnp.int32)
    owners_row, own_flag, listed = slot_flags(owner, refresh, row_index, worker_index, blocks_row)
    pick_table = (owners_row[None, :] == worker_ids[:, None]).astype(jnp.bfloat16)
    summed = lax.psum_scatter(
        partials[0].astype(jnp.float32).astype(jnp.bfloat16), "dp", scatter_dimension=0, tiled=True
    )
    outgoing = jnp.einsum(
        "wk,kxo->wxo", pick_table, summed, preferred_element_type=jnp.float32
    ).astype(jnp.bfloat16)
    gradient = lax.all_to_all(outgoing, "worker", split_axis=0, concat_axis=1, tiled=True)[0]
    stat_pair = stats[0, 0]
    old_pair = roots[0, 0]

    def refresh_both():
        return (
            newton(
                normalize(
                    STAT_DECAY * stat_pair[0] + (1.0 - STAT_DECAY) * matmul(gradient, gradient.T)
                )
            ),
            newton(
                normalize(
                    STAT_DECAY * stat_pair[1] + (1.0 - STAT_DECAY) * matmul(gradient.T, gradient)
                )
            ),
        )

    def keep_old():
        return (old_pair[0], old_pair[1])

    left_root, right_root = lax.cond(own_flag, refresh_both, keep_old)
    left_side = matmul(left_root, gradient).astype(jnp.bfloat16)
    raw_dir = matmul(left_side, right_root)
    grad_norm = jnp.sqrt(jnp.sum(jnp.square(gradient.astype(jnp.float32))))
    dir_norm = jnp.sqrt(jnp.sum(raw_dir * raw_dir) + EPSILON)
    direction = (raw_dir * (grad_norm / dir_norm)).astype(jnp.bfloat16)
    outgoing_dir = direction.reshape(workers, row_slice, block_order)
    returned_dir = lax.all_to_all(outgoing_dir, "worker", split_axis=0, concat_axis=0, tiled=True)
    return jnp.einsum(
        "wk,wxo->kxo", pick_table, returned_dir, preferred_element_type=jnp.float32
    ).astype(jnp.bfloat16)


def solution(mesh):
    in_specs = (
        P("dp", None, "worker", None),
        P("dp", "worker", None, None, None),
        P("dp", "worker", None, None, None),
        P(),
        P(),
    )
    out_specs = P("dp", "worker", None)
    return jax.shard_map(
        on_device, mesh=mesh, in_specs=in_specs, out_specs=out_specs, check_vma=False
    )
```

profile of v0, /device:TPU:6, one launch (start us, length us, event | category | flops | bytes accessed | tf_op | source)
XLA Modules:
  0.0 137.4 jit_solution(2084628540981063298)
XLA Ops:
  6.5 0.0 reduce-scatter.2.cloned.1.call-start
  6.5 0.0 copy-start
  6.5 0.7 reduce-scatter.2.cloned.1.call-update
  7.3 0.8 convert_reduce_fusion
  8.1 1.4 %and_reduce_fusion = (pred[]{:T(512)}, s32[24]{0:T(128)S(1)}) fusion(s32[24]{0:T(128)S(1)} %convert_reduce_fusion, s32[]{:T(128)S(6)} %axis_index.25, s32[192]{0:T(256)} %param.10, s32[]{:T(128)S(6)} %select_n.3), kind=kLoop, calls=%fused_computation.80 | loop fusion | flops 95 | bytes 297 | tf_op jit(solution)/shard_map/reduce_or | solution.py:44
  9.5 40.1 %reduce-scatter.2.cloned.1.call-done = bf16[24,8,512]{2,1,0:T(8,128)(2,1)} async-done(((bf16[192,8,512]{2,1,0:T(8,128)(2,1)}), bf16[24,8,512]{2,1,0:T(8,128)(2,1)}) %reduce-scatter.2.cloned.1.call-update) | async-done | bytes 196624 | tf_op jit(solution)/shard_map/reduce_scatter | solution.py:59
  49.6 1.3 convolution_convert_fusion.17
  51.0 1.1 copy.20
  52.1 13.3 %all-to-all-start = ((bf16[64,8,512]{2,1,0:T(8,128)(2,1)}), bf16[64,8,512]{2,1,0:T(8,128)(2,1)S(1)}, u32[]{:S(2)}, u32[]{:S(2)}) async-start(bf16[64,8,512]{2,1,0:T(8,128)(2,1)} %copy.20), calls=%async_computation.1 | async-start | bytes 1048576 | tf_op jit(solution)/shard_map/all_to_all | solution.py:65
  66.0 18.9 %all-to-all-done = bf16[64,8,512]{2,1,0:T(8,128)(2,1)S(1)} async-done(((bf16[64,8,512]{2,1,0:T(8,128)(2,1)}), bf16[64,8,512]{2,1,0:T(8,128)(2,1)S(1)}, u32[]{:S(2)}, u32[]{:S(2)}) %all-to-all-start) | async-done | bytes 524320 | tf_op jit(solution)/shard_map/all_to_all | solution.py:65
  84.9 0.0 copy-done
  84.9 0.1 conditional.1
  84.9 0.1 slice_bitcast_fusion
  85.0 1.4 %multiply_reduce_fusion.2 = (f32[]{:T(128)}, f32[512,512]{1,0:T(8,128)S(1)}) fusion(bf16[512,512]{1,0:T(8,128)(2,1)S(1)} %get-tuple-element.17, bf16[512,512]{1,0:T(8,128)(2,1)S(1)} %get-tuple-element.16, bf16[64,8,512]{2,1,0:T(8,128)(2,1)S(1)} %all-to-all-done), kind=kOutput, calls=%fused_computation.70 | convolution fusion | flops 537657344 | bytes 2621444 | tf_op jit(solution)/shard_map/dot_general | solution.py:14
  87.1 0.9 multiply_reduce_fusion.3
  88.7 0.1 fusion.53
  88.8 40.7 %all_to_all.14 = bf16[64,8,512]{2,1,0:T(8,128)(2,1)S(1)} all-to-all(bf16[64,8,512]{2,1,0:T(8,128)(2,1)S(1)} %fusion.53), channel_id=1, replica_groups=mesh['dp'=8,'worker'=64] {'worker'}, dimensions={0} | all-to-all | bytes 1048576 | tf_op jit(solution)/shard_map/all_to_all | solution.py:93
  129.5 0.3 convolution_convert_fusion.18
  129.8 0.7 copy.22
  (1 shorter events, 0.0 us)
Async XLA Ops:
  6.5 43.1 %reduce-scatter.2.cloned.1.call-start = ((), (), s32[]{:S(2)}) async-start(), calls=%async_computation.3 | async-start | bytes 1769472 | tf_op jit(solution)/shard_map/reduce_scatter | solution.py:59
  6.5 78.4 %copy-start = (bf16[1,1,2,512,512]{4,3,2,1,0:T(8,128)(2,1)S(1)}, bf16[1,1,2,512,512]{4,3,2,1,0:T(8,128)(2,1)}, u32[]{:S(2)}) copy-start(bf16[1,1,2,512,512]{4,3,2,1,0:T(8,128)(2,1)} %param.9) | copy-start | bytes 3145732
  52.1 32.9 %all-to-all-start = ((bf16[64,8,512]{2,1,0:T(8,128)(2,1)}), bf16[64,8,512]{2,1,0:T(8,128)(2,1)S(1)}, u32[]{:S(2)}, u32[]{:S(2)}) async-start(bf16[64,8,512]{2,1,0:T(8,128)(2,1)} %copy.20), calls=%async_computation.1 | async-start | bytes 1048576 | tf_op jit(solution)/shard_map/all_to_all | solution.py:65
Sparse Core Ops, SparseCore 0:
  10.2 39.3 reduce-scatter.1
where the time goes:
time: 138 us; the launch traced here: 137 us
  waiting for transfers between devices  59.7 us (43%)
  blocking collectives  40.7 us (29%)
  between operations  15.5 us (11%)
  starting transfers between devices  13.3 us (10%)
  other arithmetic  3.23 us (2%)
  matrix products  3.06 us (2%)
  local copies, waits for them, and re-layouts  1.89 us (1%)
    all_to_all x1, blocking collectives, on_device(): lax.all_to_all(outgoing_dir, 'worker', split_axis=0, concat_axis=0, tiled...  40.7 us
    reduce_scatter x1, waiting for transfers between devices, on_device(): lax.psum_scatter(partials[0].astype(jnp.float32).astype(jnp.bfloat16), 'd...  40.1 us
    all_to_all x1, waiting for transfers between devices, on_device(): lax.all_to_all(outgoing, 'worker', split_axis=0, concat_axis=1, tiled=True)  18.9 us
    all_to_all x1, starting transfers between devices, on_device(): lax.all_to_all(outgoing, 'worker', split_axis=0, concat_axis=1, tiled=True)  13.3 us
  transfers between devices with their start and end apart: 2, of which 2 were waited for; matrix products, arithmetic and copies ran while one was open for 2% of the time, Pallas kernels for 0%

commit v1 on v0

v1 whole, which is shorter than its diff:
```python
import functools

import jax
import jax.numpy as jnp
from jax import lax
from jax.experimental import pallas as pl
from jax.experimental.pallas import tpu as pltpu
from jax.sharding import PartitionSpec as P

ITERS = 3
STAT_DECAY = 0.9
EPSILON = 1e-06
MESH = pl.DeviceIdType.MESH
CHUNKS = ((0, 256), (256, 256))
NB = 256


def dot(a, b):
    return jnp.dot(a, b, preferred_element_type=jnp.float32)


def dot_nt(a, b):
    return lax.dot_general(a, b, (((1,), (1,)), ((), ())), preferred_element_type=jnp.float32)


def row_blocks(order):
    return [pl.ds(i, NB) for i in range(0, order, NB)]


def product(a_ref, b_ref, c_ref):
    for rows in row_blocks(a_ref.shape[0]):
        c_ref[rows, :] = dot(a_ref[rows, :], b_ref[...]).astype(c_ref.dtype)


def factor_of(m_ref, f_ref):
    order = m_ref.shape[0]
    for i in range(0, order, NB):
        rows = pl.ds(i, NB)
        row = lax.broadcasted_iota(jnp.int32, (NB, order), 0) + i
        col = lax.broadcasted_iota(jnp.int32, (NB, order), 1)
        five = jnp.where(row == col, 5.0, 0.0)
        f_ref[rows, :] = ((five - m_ref[rows, :].astype(jnp.float32)) * 0.25).astype(jnp.bfloat16)


def normalized(stat_ref, side, grams, m_ref):
    total = jnp.zeros((), jnp.float32)
    order = m_ref.shape[0]
    for rows in row_blocks(order):
        mixed = STAT_DECAY * stat_ref[side, rows, :] + (1.0 - STAT_DECAY) * grams(rows)
        stat_ref[side, rows, :] = mixed
        total = total + jnp.sum(mixed * mixed)
    scale = lax.rsqrt(jnp.full((1, order), total + EPSILON, jnp.float32))
    for rows in row_blocks(order):
        m_ref[rows, :] = (stat_ref[side, rows, :] * scale).astype(jnp.bfloat16)


def newton_pair(m, f, x, q, t):
    for it in range(ITERS):
        for s in range(2):
            factor_of(m[s], f[s])
        if it == 0:
            for s in range(2):
                x[s][...] = f[s][...]
        else:
            for s in range(2):
                product(x[s], f[s], t[s])
            for s in range(2):
                x[s][...] = t[s][...]
        if it + 1 < ITERS:
            for s in range(2):
                product(f[s], f[s], q[s])
            for s in range(2):
                product(q[s], m[s], t[s])
            for s in range(2):
                product(t[s], q[s], m[s])


def compute(fresh, g_ref, gt_ref, stat_ref, root_ref, m, f, x, q, t, raw_ref, dir_ref):
    order = g_ref.shape[0]
    normalized(stat_ref, 0, lambda rows: dot(g_ref[rows, :], gt_ref[...]), m[0])
    normalized(stat_ref, 1, lambda rows: dot(gt_ref[rows, :], g_ref[...]), m[1])
    newton_pair(m, f, x, q, t)
    take = jnp.full((1, order), fresh, jnp.int32) > 0
    for s in range(2):
        for rows in row_blocks(order):
            x[s][rows, :] = jnp.where(
                take, x[s][rows, :].astype(jnp.float32), root_ref[s, rows, :].astype(jnp.float32)
            ).astype(jnp.bfloat16)
    product(x[0], g_ref, t[0])
    grad_sq = jnp.zeros((), jnp.float32)
    raw_sq = jnp.zeros((), jnp.float32)
    for rows in row_blocks(order):
        raw = dot(t[0][rows, :], x[1][...])
        raw_ref[rows, :] = raw
        raw_sq = raw_sq + jnp.sum(raw * raw)
        g32 = g_ref[rows, :].astype(jnp.float32)
        grad_sq = grad_sq + jnp.sum(g32 * g32)
    scale = jnp.sqrt(jnp.full((1, order), grad_sq, jnp.float32)) / jnp.sqrt(
        jnp.full((1, order), raw_sq + EPSILON, jnp.float32)
    )
    for i in range(0, order, NB):
        d = (raw_ref[pl.ds(i, NB), :] * scale).reshape(NB // 8, 8, order)
        dir_ref[pl.ds(i // 8, NB // 8)] = d.astype(jnp.bfloat16)


def kernel(
    part_ref, stats_hbm, roots_hbm, owner_ref, refresh_ref, out_ref,
    own, pair, recvx, summed, outgoing, gath, ret, dirs, slot_ref,
    g_ref, gt_ref, stat_ref, root_ref, m0, m1, f0, f1, x0, x1, q0, q1, t0, t1, raw_ref,
    load_sem, own_sem, pair_send, pair_recv, x_send, x_recv, a_send, a_recv, r_send, r_recv,
):
    chips, blocks, rows8, order = own.shape
    workers = gath.shape[0]
    g, w = lax.axis_index("dp"), lax.axis_index("worker")
    x, c = lax.div(g, 2), lax.rem(g, 2)
    nc = len(CHUNKS)

    def other_worker(i):
        return lax.rem(w + i, workers)

    barrier = pltpu.get_barrier_semaphore()
    pl.semaphore_signal(barrier, inc=1, device_id=(x * 2 + 1 - c, w), device_id_type=MESH)
    for i in range(1, chips):
        to = lax.rem(x + i, chips) * 2 + c
        pl.semaphore_signal(barrier, inc=1, device_id=(to, w), device_id_type=MESH)

    def greet(i, carry):
        pl.semaphore_signal(barrier, inc=1, device_id=(g, other_worker(i)), device_id_type=MESH)
        return carry

    lax.fori_loop(1, workers, greet, 0)

    def own_copy(j, t):
        cols = pl.ds(*CHUNKS[j])
        return pltpu.make_async_copy(
            part_ref.at[t, c, :, :, cols], own.at[t, :, :, cols], own_sem.at[j, t]
        )

    def pair_copy(j, t):
        cols = pl.ds(*CHUNKS[j])
        return pltpu.make_async_remote_copy(
            part_ref.at[t, 1 - c, :, :, cols], pair.at[t, :, :, cols],
            pair_send.at[j, t], pair_recv.at[j, t],
            device_id=(x * 2 + 1 - c, w), device_id_type=MESH,
        )

    def x_copy(j, i):
        cols = pl.ds(*CHUNKS[j])
        to = lax.rem(x + i, chips)
        return pltpu.make_async_remote_copy(
            own.at[to, :, :, cols], recvx.at[i - 1, :, :, cols],
            x_send.at[j, i - 1], x_recv.at[j, i - 1],
            device_id=(to * 2 + c, w), device_id_type=MESH,
        )

    def a_copy(j, to):
        cols = pl.ds(*CHUNKS[j])
        return pltpu.make_async_remote_copy(
            outgoing.at[to, :, cols], gath.at[w, :, cols], a_send.at[j], a_recv.at[j],
            device_id=(g, to), device_id_type=MESH,
        )

    def a_all(j):
        cols, rest = pl.ds(*CHUNKS[j]), pl.ds(0, workers - 1)
        return pltpu.make_async_remote_copy(
            outgoing.at[rest, :, cols], gath.at[rest, :, cols], a_send.at[j], a_recv.at[j],
            device_id=(g, w), device_id_type=MESH,
        )

    def r_copy(to):
        return pltpu.make_async_remote_copy(
            dirs.at[to], ret.at[w], r_send, r_recv, device_id=(g, to), device_id_type=MESH
        )

    def r_all():
        rest = pl.ds(0, workers - 1)
        return pltpu.make_async_remote_copy(
            dirs.at[rest], ret.at[rest], r_send, r_recv, device_id=(g, w), device_id_type=MESH
        )

    hops = (2, 1, 3, 0)
    for j in range(nc):
        for i in hops:
            own_copy(j, lax.rem(x + i, chips)).start()
    stat_load = pltpu.make_async_copy(stats_hbm, stat_ref, load_sem.at[0])
    root_load = pltpu.make_async_copy(roots_hbm, root_ref, load_sem.at[1])
    stat_load.start()
    root_load.start()
    pl.semaphore_wait(barrier, chips + workers - 1)
    for j in range(nc):
        for i in hops:
            pair_copy(j, lax.rem(x + i, chips)).start()

    step = 8
    for j in range(nc):
        cols = pl.ds(*CHUNKS[j])
        for i in hops:
            t = lax.rem(x + i, chips)
            own_copy(j, t).wait()
            pair_copy(j, t).wait_recv()
            if i == 0:
                continue
            for k in range(0, blocks, step):
                ks = pl.ds(k, step)
                own[t, ks, :, cols] = (
                    own[t, ks, :, cols].astype(jnp.float32) + pair[t, ks, :, cols].astype(jnp.float32)
                ).astype(jnp.bfloat16)
            x_copy(j, i).start()

    first = g * blocks

    def find_slot(t, carry):
        slot = jnp.int32(0)
        for k in range(blocks):
            slot = jnp.where(owner_ref[first + k] == t, k, slot)
        slot_ref[t] = slot
        return carry

    lax.fori_loop(0, workers, find_slot, 0)

    for j in range(nc):
        cols = pl.ds(*CHUNKS[j])
        for i in range(1, chips):
            x_copy(j, i).wait_recv()
        for k in range(0, blocks, step):
            ks = pl.ds(k, step)
            total = own[x, ks, :, cols].astype(jnp.float32) + pair[x, ks, :, cols].astype(jnp.float32)
            for i in range(chips - 1):
                total = total + recvx[i, ks, :, cols].astype(jnp.float32)
            summed[ks, :, cols] = total.astype(jnp.bfloat16)

        def pack(i, carry):
            to = other_worker(i)
            outgoing[to, :, cols] = summed[slot_ref[to], :, cols]
            a_copy(j, to).start()
            return carry

        lax.fori_loop(1, workers, pack, 0)
        gath[w, :, cols] = summed[slot_ref[w], :, cols]

    mine = first + slot_ref[w]

    def is_listed(i, carry):
        return carry + jnp.where(refresh_ref[i] == mine, 1, 0)

    fresh = lax.fori_loop(0, refresh_ref.shape[0], is_listed, jnp.int32(0))

    for j in range(nc):
        cols = pl.ds(*CHUNKS[j])
        a_all(j).wait_recv()
        for i in range(0, workers, 16):
            piece = gath[pl.ds(i, 16), :, cols].astype(jnp.float32).reshape(16 * rows8, CHUNKS[j][1])
            g_ref[pl.ds(i * rows8, 16 * rows8), cols] = piece.astype(jnp.bfloat16)
        gt_ref[cols, :] = g_ref[:, cols].T
    stat_load.wait()
    root_load.wait()
    compute(
        fresh, g_ref, gt_ref, stat_ref, root_ref, (m0, m1), (f0, f1), (x0, x1), (q0, q1), (t0, t1),
        raw_ref, dirs,
    )

    def send_back(i, carry):
        r_copy(other_worker(i)).start()
        return carry

    lax.fori_loop(1, workers, send_back, 0)
    ret[w] = dirs[w]
    for j in range(nc):
        for i in range(chips):
            pair_copy(j, i).wait_send()
        for i in range(1, chips):
            x_copy(j, i).wait_send()
        a_all(j).wait_send()
    r_all().wait_recv()
    for k in range(blocks):
        out_ref[k] = ret[owner_ref[first + k]]
    r_all().wait_send()


def on_device(partials, stats, roots, owner, refresh):
    workers, replicas = lax.axis_size("worker"), lax.axis_size("dp")
    _, total, rows, order = partials.shape
    chips, blocks = replicas // 2, total // replicas
    nc = len(CHUNKS)
    bf, dma = functools.partial(pltpu.VMEM, dtype=jnp.bfloat16), pltpu.SemaphoreType.DMA
    square = bf((order, order))
    return pl.pallas_call(
        kernel,
        out_shape=jax.ShapeDtypeStruct((blocks, rows, order), jnp.bfloat16),
        in_specs=[pl.BlockSpec(memory_space=pl.ANY)] * 3
        + [pl.BlockSpec(memory_space=pltpu.SMEM)] * 2,
        out_specs=pl.BlockSpec(memory_space=pltpu.VMEM),
        scratch_shapes=[
            bf((chips, blocks, rows, order)),
            bf((chips, blocks, rows, order)),
            bf((chips - 1, blocks, rows, order)),
            bf((blocks, rows, order)),
            bf((workers, rows, order)),
            bf((workers, rows, order)),
            bf((workers, rows, order)),
            bf((workers, rows, order)),
            pltpu.SMEM((workers,), jnp.int32),
            square,
            square,
            pltpu.VMEM((2, order, order), jnp.float32),
            bf((2, order, order)),
        ]
        + [square] * 10
        + [
            pltpu.VMEM((order, order), jnp.float32),
            dma((2,)),
            dma((nc, chips)),
            dma((nc, chips)),
            dma((nc, chips)),
            dma((nc, chips - 1)),
            dma((nc, chips - 1)),
            dma((nc,)),
            dma((nc,)),
            dma,
            dma,
        ],
        compiler_params=pltpu.CompilerParams(
            collective_id=0, has_side_effects=True, vmem_limit_bytes=56 * 2**20
        ),
    )(
        partials.reshape(chips, 2, blocks, rows, order),
        stats.reshape(2, order, order),
        roots.reshape(2, order, order),
        owner,
        refresh,
    )


def solution(mesh):
    in_specs = (
        P("dp", None, "worker", None),
        P("dp", "worker", None, None, None),
        P("dp", "worker", None, None, None),
        P(),
        P(),
    )
    return jax.shard_map(
        on_device,
        mesh=mesh,
        in_specs=in_specs,
        out_specs=P("dp", "worker", None),
        check_vma=False,
    )
```

time: 138 us -> 72 us (0.52)
  the two profiles are of different devices: /device:TPU:6 before, /device:TPU:8 now
where the time goes in v1:
time: 72 us; the launch traced here: 71.8 us
  Pallas kernels  70.2 us (98%)
  local copies, waits for them, and re-layouts  1.62 us (2%)
    pallas_call x1, Pallas kernels, on_device(): pl.pallas_call(kernel, out_shape=jax.ShapeDtypeStruct((blocks, rows, orde...  70.2 us
    unnamed x1, local copies, waits for them, and re-layouts  1.62 us

profile of v1, /device:TPU:8, one launch (start us, length us, event | category | flops | bytes accessed | tf_op | source)
XLA Modules:
  0.0 71.8 jit_solution(12757679736702671770)
XLA Ops:
  0.0 70.2 %shard_map.55 = bf16[24,8,512]{2,1,0:T(8,128)(2,1)} custom-call(bf16[4,2,24,8,512]{4,3,2,1,0:T(8,128)(2,1)} %bitcast.4, f32[2,512,512]{2,1,0:T(8,128)} %bitcast.3, bf16[2,512,512]{2,1,0:T(8,128)(2,1)} %bitcast.5, s32[192]{0:T(256)} %owner_ref.1, s32[64]{0:T(128)} %refresh_ref.1), custom_call_target="tpu_custom_call" | custom-call | tf_op jit(solution)/shard_map/pallas_call | solution.py:287
  70.2 1.6 %copy.7 = bf16[24,8,512]{2,1,0:T(8,128)(2,1)} copy(bf16[24,8,512]{2,1,0:T(8,128)(2,1)} %shard_map.55) | data formatting | bytes 393216

commit v2 on v1

--- a/solution.py
+++ b/solution.py
@@ -11,7 +11,8 @@
 STAT_DECAY = 0.9
 EPSILON = 1e-06
 MESH = pl.DeviceIdType.MESH
-CHUNKS = ((0, 256), (256, 256))
+SIDE = 8
+CHUNKS = ((0, 128), (128, 128), (256, 256))
 NB = 256
 
 
@@ -107,7 +108,7 @@
     part_ref, stats_hbm, roots_hbm, owner_ref, refresh_ref, out_ref,
     own, pair, recvx, summed, outgoing, gath, ret, dirs, slot_ref,
     g_ref, gt_ref, stat_ref, root_ref, m0, m1, f0, f1, x0, x1, q0, q1, t0, t1, raw_ref,
-    load_sem, own_sem, pair_send, pair_recv, x_send, x_recv, a_send, a_recv, r_send, r_recv,
+    load_sem, own_sem, pair_send, pair_recv, x_send, x_recv, a_send, a_recv, r_send, r_recv, line_sem,
 ):
     chips, blocks, rows8, order = own.shape
     workers = gath.shape[0]
@@ -124,11 +125,13 @@
         to = lax.rem(x + i, chips) * 2 + c
         pl.semaphore_signal(barrier, inc=1, device_id=(to, w), device_id_type=MESH)
 
-    def greet(i, carry):
-        pl.semaphore_signal(barrier, inc=1, device_id=(g, other_worker(i)), device_id_type=MESH)
-        return carry
-
-    lax.fori_loop(1, workers, greet, 0)
+    side = SIDE
+    z, y = lax.div(w, side), lax.rem(w, side)
+    for i in range(1, side):
+        beside = z * side + lax.rem(y + i, side)
+        above = lax.rem(z + i, side) * side + y
+        pl.semaphore_signal(barrier, inc=1, device_id=(g, beside), device_id_type=MESH)
+        pl.semaphore_signal(barrier, inc=1, device_id=(g, above), device_id_type=MESH)
 
     def own_copy(j, t):
         cols = pl.ds(*CHUNKS[j])
@@ -186,10 +189,13 @@
     root_load = pltpu.make_async_copy(roots_hbm, root_ref, load_sem.at[1])
     stat_load.start()
     root_load.start()
-    pl.semaphore_wait(barrier, chips + workers - 1)
+    pl.semaphore_wait(barrier, chips + 2 * (side - 1))
     for j in range(nc):
         for i in hops:
             pair_copy(j, lax.rem(x + i, chips)).start()
+    for i in range(1, side):
+        above = lax.rem(z + i, side) * side + y
+        pl.semaphore_signal(line_sem, inc=1, device_id=(g, above), device_id_type=MESH)
 
     step = 8
     for j in range(nc):
@@ -217,6 +223,7 @@
         return carry
 
     lax.fori_loop(0, workers, find_slot, 0)
+    pl.semaphore_wait(line_sem, side - 1)
 
     for j in range(nc):
         cols = pl.ds(*CHUNKS[j])
@@ -259,8 +266,10 @@
         raw_ref, dirs,
     )
 
+    turn = 1 - 2 * lax.rem(z + y, 2)
+
     def send_back(i, carry):
-        r_copy(other_worker(i)).start()
+        r_copy(lax.rem(w + turn * i + workers, workers)).start()
         return carry
 
     lax.fori_loop(1, workers, send_back, 0)
@@ -318,6 +327,7 @@
             dma((nc,)),
             dma,
             dma,
+            pltpu.SemaphoreType.REGULAR,
         ],
         compiler_params=pltpu.CompilerParams(
             collective_id=0, has_side_effects=True, vmem_limit_bytes=56 * 2**20

time: 72 us -> 61.5 us (0.85)
  Pallas kernels: 70.2 us -> 59.8 us
    pallas_call x1, Pallas kernels: 70.2 us -> 59.8 us  [on_device(): pl.pallas_call(kernel, out_shape=jax.ShapeDtypeStruct((blocks, rows, orde...]
where the time goes in v2:
time: 61.5 us; the launch traced here: 61.4 us
  Pallas kernels  59.8 us (97%)
  local copies, waits for them, and re-layouts  1.62 us (3%)
    pallas_call x1, Pallas kernels, on_device(): pl.pallas_call(kernel, out_shape=jax.ShapeDtypeStruct((blocks, rows, orde...  59.8 us
    unnamed x1, local copies, waits for them, and re-layouts  1.62 us

profile of v2, /device:TPU:8, one launch (start us, length us, event | category | flops | bytes accessed | tf_op | source)
XLA Modules:
  0.0 61.4 jit_solution(16342947432741190000)
XLA Ops:
  0.0 59.8 %shard_map.55 = bf16[24,8,512]{2,1,0:T(8,128)(2,1)} custom-call(bf16[4,2,24,8,512]{4,3,2,1,0:T(8,128)(2,1)} %bitcast.4, f32[2,512,512]{2,1,0:T(8,128)} %bitcast.3, bf16[2,512,512]{2,1,0:T(8,128)(2,1)} %bitcast.5, s32[192]{0:T(256)} %owner_ref.1, s32[64]{0:T(128)} %refresh_ref.1), custom_call_target="tpu_custom_call" | custom-call | tf_op jit(solution)/shard_map/pallas_call | solution.py:296
  59.8 1.6 %copy.7 = bf16[24,8,512]{2,1,0:T(8,128)(2,1)} copy(bf16[24,8,512]{2,1,0:T(8,128)(2,1)} %shard_map.55) | data formatting | bytes 393216

commit v3 on v2

--- a/solution.py
+++ b/solution.py
@@ -12,8 +12,9 @@
 EPSILON = 1e-06
 MESH = pl.DeviceIdType.MESH
 SIDE = 8
+BACK = ((0, 0), (0, 1), (1, 0), (0, 2), (0, 3), (1, 1), (1, 2), (1, 3))
 CHUNKS = ((0, 128), (128, 128), (256, 256))
-NB = 256
+NB = 512
 
 
 def dot(a, b):
@@ -33,82 +34,82 @@
         c_ref[rows, :] = dot(a_ref[rows, :], b_ref[...]).astype(c_ref.dtype)
 
 
-def factor_of(m_ref, f_ref):
+def put(rows, m32, m_ref, f_ref):
+    shape = m32.shape
+    m = m32.astype(jnp.bfloat16)
+    row = lax.broadcasted_iota(jnp.int32, shape, 0) + rows.start
+    col = lax.broadcasted_iota(jnp.int32, shape, 1)
+    five = jnp.where(row == col, 5.0, 0.0)
+    m_ref[rows, :] = m
+    f_ref[rows, :] = ((five - m.astype(jnp.float32)) * 0.25).astype(jnp.bfloat16)
+
+
+def normalized(stat_ref, side, left, right, m_ref, f_ref):
     order = m_ref.shape[0]
+    total = jnp.zeros((1, order), jnp.float32)
+    for rows in row_blocks(order):
+        mixed = STAT_DECAY * stat_ref[side, rows, :] + (1.0 - STAT_DECAY) * dot(left[rows, :], right[...])
+        stat_ref[side, rows, :] = mixed
+        total = total + jnp.sum(mixed * mixed, axis=0, keepdims=True)
+    scale = lax.rsqrt(jnp.full((1, order), jnp.sum(total) + EPSILON, jnp.float32))
+    for rows in row_blocks(order):
+        put(rows, stat_ref[side, rows, :] * scale, m_ref, f_ref)
+
+
+def compute(take, g_ref, gt_ref, stat_ref, root_ref, m, f, x, q, t, raw_ref, dir_ref):
+    order = g_ref.shape[0]
+    normalized(stat_ref, 0, g_ref, gt_ref, m[0], f[0])
+    normalized(stat_ref, 1, gt_ref, g_ref, m[1], f[1])
+    held = [f[0], f[1]]
+    factor = [f[0], f[1]]
+    spare = [[x[0], t[0]], [x[1], t[1]]]
+    for it in range(ITERS - 1):
+        if it > 0:
+            for s in range(2):
+                new = spare[s].pop(0)
+                product(held[s], factor[s], new)
+                spare[s].append(held[s])
+                held[s] = new
+        y = [spare[s][0] for s in range(2)]
+        for s in range(2):
+            product(factor[s], factor[s], q[s])
+        for s in range(2):
+            product(q[s], m[s], y[s])
+        later = [raw_ref.at[s] for s in range(2)] if it == 0 else factor
+        for s in range(2):
+            for rows in row_blocks(order):
+                put(rows, dot(y[s][rows, :], q[s][...]), m[s], later[s])
+        factor = later
+    for s in range(2):
+        new = spare[s].pop(0)
+        for rows in row_blocks(order):
+            root = dot(held[s][rows, :], factor[s][...])
+            old = root_ref[s, rows, :].astype(jnp.float32)
+            new[rows, :] = jnp.where(take, root, old).astype(jnp.bfloat16)
+        spare[s].append(held[s])
+        held[s] = new
+    product(held[0], g_ref, q[0])
+    grad_sq = jnp.zeros((1, order), jnp.float32)
+    raw_sq = jnp.zeros((1, order), jnp.float32)
+    for rows in row_blocks(order):
+        raw = dot(q[0][rows, :], held[1][...])
+        stat_ref[0, rows, :] = raw
+        raw_sq = raw_sq + jnp.sum(raw * raw, axis=0, keepdims=True)
+        g32 = g_ref[rows, :].astype(jnp.float32)
+        grad_sq = grad_sq + jnp.sum(g32 * g32, axis=0, keepdims=True)
+    scale = jnp.sqrt(jnp.full((1, order), jnp.sum(grad_sq), jnp.float32)) / jnp.sqrt(
+        jnp.full((1, order), jnp.sum(raw_sq) + EPSILON, jnp.float32)
+    )
     for i in range(0, order, NB):
-        rows = pl.ds(i, NB)
-        row = lax.broadcasted_iota(jnp.int32, (NB, order), 0) + i
-        col = lax.broadcasted_iota(jnp.int32, (NB, order), 1)
-        five = jnp.where(row == col, 5.0, 0.0)
-        f_ref[rows, :] = ((five - m_ref[rows, :].astype(jnp.float32)) * 0.25).astype(jnp.bfloat16)
-
-
-def normalized(stat_ref, side, grams, m_ref):
-    total = jnp.zeros((), jnp.float32)
-    order = m_ref.shape[0]
-    for rows in row_blocks(order):
-        mixed = STAT_DECAY * stat_ref[side, rows, :] + (1.0 - STAT_DECAY) * grams(rows)
-        stat_ref[side, rows, :] = mixed
-        total = total + jnp.sum(mixed * mixed)
-    scale = lax.rsqrt(jnp.full((1, order), total + EPSILON, jnp.float32))
-    for rows in row_blocks(order):
-        m_ref[rows, :] = (stat_ref[side, rows, :] * scale).astype(jnp.bfloat16)
-
-
-def newton_pair(m, f, x, q, t):
-    for it in range(ITERS):
-        for s in range(2):
-            factor_of(m[s], f[s])
-        if it == 0:
-            for s in range(2):
-                x[s][...] = f[s][...]
-        else:
-            for s in range(2):
-                product(x[s], f[s], t[s])
-            for s in range(2):
-                x[s][...] = t[s][...]
-        if it + 1 < ITERS:
-            for s in range(2):
-                product(f[s], f[s], q[s])
-            for s in range(2):
-                product(q[s], m[s], t[s])
-            for s in range(2):
-                product(t[s], q[s], m[s])
-
-
-def compute(fresh, g_ref, gt_ref, stat_ref, root_ref, m, f, x, q, t, raw_ref, dir_ref):
-    order = g_ref.shape[0]
-    normalized(stat_ref, 0, lambda rows: dot(g_ref[rows, :], gt_ref[...]), m[0])
-    normalized(stat_ref, 1, lambda rows: dot(gt_ref[rows, :], g_ref[...]), m[1])
-    newton_pair(m, f, x, q, t)
-    take = jnp.full((1, order), fresh, jnp.int32) > 0
-    for s in range(2):
-        for rows in row_blocks(order):
-            x[s][rows, :] = jnp.where(
-                take, x[s][rows, :].astype(jnp.float32), root_ref[s, rows, :].astype(jnp.float32)
-            ).astype(jnp.bfloat16)
-    product(x[0], g_ref, t[0])
-    grad_sq = jnp.zeros((), jnp.float32)
-    raw_sq = jnp.zeros((), jnp.float32)
-    for rows in row_blocks(order):
-        raw = dot(t[0][rows, :], x[1][...])
-        raw_ref[rows, :] = raw
-        raw_sq = raw_sq + jnp.sum(raw * raw)
-        g32 = g_ref[rows, :].astype(jnp.float32)
-        grad_sq = grad_sq + jnp.sum(g32 * g32)
-    scale = jnp.sqrt(jnp.full((1, order), grad_sq, jnp.float32)) / jnp.sqrt(
-        jnp.full((1, order), raw_sq + EPSILON, jnp.float32)
-    )
-    for i in range(0, order, NB):
-        d = (raw_ref[pl.ds(i, NB), :] * scale).reshape(NB // 8, 8, order)
+        d = (stat_ref[0, pl.ds(i, NB), :] * scale).reshape(NB // 8, 8, order)
         dir_ref[pl.ds(i // 8, NB // 8)] = d.astype(jnp.bfloat16)
 
 
 def kernel(
-    part_ref, stats_hbm, roots_hbm, owner_ref, refresh_ref, out_ref,
-    own, pair, recvx, summed, outgoing, gath, ret, dirs, slot_ref,
+    part_ref, stats_hbm, roots_hbm, owner_hbm, refresh_hbm, out_ref,
+    own, pair, recvx, summed, outgoing, gath, ret, dirs, slot_ref, owner_ref, refresh_ref,
     g_ref, gt_ref, stat_ref, root_ref, m0, m1, f0, f1, x0, x1, q0, q1, t0, t1, raw_ref,
-    load_sem, own_sem, pair_send, pair_recv, x_send, x_recv, a_send, a_recv, r_send, r_recv, line_sem,
+    load_sem, own_sem, pair_send, pair_recv, x_send, x_recv, a_send, a_recv, r_send, r_recv, row_sem,
 ):
     chips, blocks, rows8, order = own.shape
     workers = gath.shape[0]
@@ -182,6 +183,10 @@
         )
 
     hops = (2, 1, 3, 0)
+    owner_load = pltpu.make_async_copy(owner_hbm, owner_ref, load_sem.at[2])
+    refresh_load = pltpu.make_async_copy(refresh_hbm, refresh_ref, load_sem.at[3])
+    owner_load.start()
+    refresh_load.start()
     for j in range(nc):
         for i in hops:
             own_copy(j, lax.rem(x + i, chips)).start()
@@ -195,10 +200,12 @@
             pair_copy(j, lax.rem(x + i, chips)).start()
     for i in range(1, side):
         above = lax.rem(z + i, side) * side + y
-        pl.semaphore_signal(line_sem, inc=1, device_id=(g, above), device_id_type=MESH)
+        pl.semaphore_signal(row_sem.at[z], inc=1, device_id=(g, above), device_id_type=MESH)
 
     step = 8
-    for j in range(nc):
+    first = g * blocks
+
+    def add_pair(j):
         cols = pl.ds(*CHUNKS[j])
         for i in hops:
             t = lax.rem(x + i, chips)
@@ -213,17 +220,25 @@
                 ).astype(jnp.bfloat16)
             x_copy(j, i).start()
 
-    first = g * blocks
-
-    def find_slot(t, carry):
-        slot = jnp.int32(0)
-        for k in range(blocks):
-            slot = jnp.where(owner_ref[first + k] == t, k, slot)
-        slot_ref[t] = slot
-        return carry
-
-    lax.fori_loop(0, workers, find_slot, 0)
-    pl.semaphore_wait(line_sem, side - 1)
+    def find_slots():
+        owners = [owner_ref[first + k] for k in range(blocks)]
+
+        def find(t, carry):
+            slot = jnp.int32(0)
+            for k in range(blocks):
+                slot = jnp.where(owners[k] == t, k, slot)
+            slot_ref[t] = slot
+            return carry
+
+        lax.fori_loop(0, workers, find, 0, unroll=2)
+
+    add_pair(0)
+    add_pair(1)
+    owner_load.wait()
+    refresh_load.wait()
+    find_slots()
+    for j in range(2, nc):
+        add_pair(j)
 
     for j in range(nc):
         cols = pl.ds(*CHUNKS[j])
@@ -236,13 +251,24 @@
                 total = total + recvx[i, ks, :, cols].astype(jnp.float32)
             summed[ks, :, cols] = total.astype(jnp.bfloat16)
 
-        def pack(i, carry):
-            to = other_worker(i)
+        def send(row, i):
+            to = row * side + lax.rem(y + i, side)
             outgoing[to, :, cols] = summed[slot_ref[to], :, cols]
             a_copy(j, to).start()
+
+        def send_own_row(i, carry):
+            send(z, i)
             return carry
 
-        lax.fori_loop(1, workers, pack, 0)
+        def send_row(k, carry):
+            row = lax.rem(z + k, side)
+            if j == 0:
+                pl.semaphore_wait(row_sem.at[row], 1)
+            lax.fori_loop(0, side, lambda i, c: (send(row, i), c)[1], 0)
+            return carry
+
+        lax.fori_loop(1, side, send_own_row, 0)
+        lax.fori_loop(1, side, send_row, 0)
         gath[w, :, cols] = summed[slot_ref[w], :, cols]
 
     mine = first + slot_ref[w]
@@ -261,18 +287,23 @@
         gt_ref[cols, :] = g_ref[:, cols].T
     stat_load.wait()
     root_load.wait()
+    take = jnp.full((1, order), fresh, jnp.int32) > 0
     compute(
-        fresh, g_ref, gt_ref, stat_ref, root_ref, (m0, m1), (f0, f1), (x0, x1), (q0, q1), (t0, t1),
+        take, g_ref, gt_ref, stat_ref, root_ref, (m0, m1), (f0, f1), (x0, x1), (q0, q1), (t0, t1),
         raw_ref, dirs,
     )
 
     turn = 1 - 2 * lax.rem(z + y, 2)
 
-    def send_back(i, carry):
-        r_copy(lax.rem(w + turn * i + workers, workers)).start()
-        return carry
-
-    lax.fori_loop(1, workers, send_back, 0)
+    def send_back(row):
+        def one(i, carry):
+            r_copy(row * side + lax.rem(y + turn * i + side, side)).start()
+            return carry
+
+        lax.fori_loop(jnp.where(row == z, 1, 0), side, one, 0)
+
+    for half, k in BACK:
+        send_back(4 * half + lax.rem(z + k, 4))
     ret[w] = dirs[w]
     for j in range(nc):
         for i in range(chips):
@@ -296,8 +327,7 @@
     return pl.pallas_call(
         kernel,
         out_shape=jax.ShapeDtypeStruct((blocks, rows, order), jnp.bfloat16),
-        in_specs=[pl.BlockSpec(memory_space=pl.ANY)] * 3
-        + [pl.BlockSpec(memory_space=pltpu.SMEM)] * 2,
+        in_specs=[pl.BlockSpec(memory_space=pltpu.HBM)] * 5,
         out_specs=pl.BlockSpec(memory_space=pltpu.VMEM),
         scratch_shapes=[
             bf((chips, blocks, rows, order)),
@@ -309,6 +339,8 @@
             bf((workers, rows, order)),
             bf((workers, rows, order)),
             pltpu.SMEM((workers,), jnp.int32),
+            pltpu.SMEM(owner.shape, jnp.int32),
+            pltpu.SMEM(refresh.shape, jnp.int32),
             square,
             square,
             pltpu.VMEM((2, order, order), jnp.float32),
@@ -316,8 +348,8 @@
         ]
         + [square] * 10
         + [
-            pltpu.VMEM((order, order), jnp.float32),
-            dma((2,)),
+            bf((2, order, order)),
+            dma((4,)),
             dma((nc, chips)),
             dma((nc, chips)),
             dma((nc, chips)),
@@ -327,10 +359,10 @@
             dma((nc,)),
             dma,
             dma,
-            pltpu.SemaphoreType.REGULAR,
+            pltpu.SemaphoreType.REGULAR((SIDE,)),
         ],
         compiler_params=pltpu.CompilerParams(
-            collective_id=0, has_side_effects=True, vmem_limit_bytes=56 * 2**20
+            collective_id=0, has_side_effects=True, vmem_limit_bytes=53 * 2**20 + 2**19
         ),
     )(
         partials.reshape(chips, 2, blocks, rows, order),

time: 61.5 us -> 59.8 us (0.972)
  Pallas kernels: 59.8 us -> 57.6 us
    pallas_call x1, Pallas kernels: 59.8 us -> 57.6 us  [on_device(): pl.pallas_call(kernel, out_shape=jax.ShapeDtypeStruct((blocks, rows, orde...]
    unnamed x1 -> x5, local copies, waits for them, and re-layouts: 1.62 us -> 2.01 us
where the time goes in v3:
time: 59.8 us; the launch traced here: 59.6 us
  Pallas kernels  57.6 us (96%)
  local copies, waits for them, and re-layouts  2.01 us (3%)
    pallas_call x1, Pallas kernels, on_device(): pl.pallas_call(kernel, out_shape=jax.ShapeDtypeStruct((blocks, rows, orde...  57.6 us
    unnamed x5, local copies, waits for them, and re-layouts  2.01 us

profile of v3, /device:TPU:8, one launch (start us, length us, event | category | flops | bytes accessed | tf_op | source)
XLA Modules:
  0.0 59.6 jit_solution(18285195031977218269)
XLA Ops:
  0.0 0.0 copy-start
  0.0 0.7 %copy-done = s32[192]{0:T(256)S(1)} copy-done((s32[192]{0:T(256)S(1)}, s32[192]{0:T(256)}, u32[]{:S(2)}) %copy-start) | copy-done | bytes 792
  0.7 0.0 copy-start.1
  0.7 0.7 %copy-done.1 = s32[64]{0:T(128)S(1)} copy-done((s32[64]{0:T(128)S(1)}, s32[64]{0:T(128)}, u32[]{:S(2)}) %copy-start.1) | copy-done | bytes 280
  1.3 57.6 %shard_map.55 = bf16[24,8,512]{2,1,0:T(8,128)(2,1)S(1)} custom-call(bf16[4,2,24,8,512]{4,3,2,1,0:T(8,128)(2,1)} %bitcast.4, f32[2,512,512]{2,1,0:T(8,128)} %bitcast.3, bf16[2,512,512]{2,1,0:T(8,128)(2,1)} %bitcast.5, s32[192]{0:T(256)S(1)} %copy-done, s32[64]{0:T(128)S(1)} %copy-done.1), custom_call_target="tpu_custom_call" | custom-call | tf_op jit(solution)/shard_map/pallas_call | solution.py:327
  58.9 0.7 %copy.7 = bf16[24,8,512]{2,1,0:T(8,128)(2,1)} copy(bf16[24,8,512]{2,1,0:T(8,128)(2,1)S(1)} %shard_map.55) | data formatting | bytes 393216
Async XLA Ops:
  0.0 0.7 %copy-start = (s32[192]{0:T(256)S(1)}, s32[192]{0:T(256)}, u32[]{:S(2)}) copy-start(s32[192]{0:T(256)} %owner_hbm.1) | copy-start | bytes 2308
  0.7 0.7 %copy-start.1 = (s32[64]{0:T(128)S(1)}, s32[64]{0:T(128)}, u32[]{:S(2)}) copy-start(s32[64]{0:T(128)} %refresh_hbm.1) | copy-start | bytes 772

commit v4 on v3

--- a/solution.py
+++ b/solution.py
@@ -134,10 +134,10 @@
         pl.semaphore_signal(barrier, inc=1, device_id=(g, beside), device_id_type=MESH)
         pl.semaphore_signal(barrier, inc=1, device_id=(g, above), device_id_type=MESH)
 
-    def own_copy(j, t):
+    def own_copy(j):
         cols = pl.ds(*CHUNKS[j])
         return pltpu.make_async_copy(
-            part_ref.at[t, c, :, :, cols], own.at[t, :, :, cols], own_sem.at[j, t]
+            part_ref.at[:, c, :, :, cols], own.at[:, :, :, cols], own_sem.at[j]
         )
 
     def pair_copy(j, t):
@@ -183,21 +183,17 @@
         )
 
     hops = (2, 1, 3, 0)
+    own_copy(0).start()
+    pl.semaphore_wait(barrier, chips + 2 * (side - 1))
+    for j in range(nc):
+        for i in hops:
+            pair_copy(j, lax.rem(x + i, chips)).start()
+        if j > 0:
+            own_copy(j).start()
     owner_load = pltpu.make_async_copy(owner_hbm, owner_ref, load_sem.at[2])
     refresh_load = pltpu.make_async_copy(refresh_hbm, refresh_ref, load_sem.at[3])
     owner_load.start()
     refresh_load.start()
-    for j in range(nc):
-        for i in hops:
-            own_copy(j, lax.rem(x + i, chips)).start()
-    stat_load = pltpu.make_async_copy(stats_hbm, stat_ref, load_sem.at[0])
-    root_load = pltpu.make_async_copy(roots_hbm, root_ref, load_sem.at[1])
-    stat_load.start()
-    root_load.start()
-    pl.semaphore_wait(barrier, chips + 2 * (side - 1))
-    for j in range(nc):
-        for i in hops:
-            pair_copy(j, lax.rem(x + i, chips)).start()
     for i in range(1, side):
         above = lax.rem(z + i, side) * side + y
         pl.semaphore_signal(row_sem.at[z], inc=1, device_id=(g, above), device_id_type=MESH)
@@ -207,9 +203,9 @@
 
     def add_pair(j):
         cols = pl.ds(*CHUNKS[j])
+        own_copy(j).wait()
         for i in hops:
             t = lax.rem(x + i, chips)
-            own_copy(j, t).wait()
             pair_copy(j, t).wait_recv()
             if i == 0:
                 continue
@@ -239,6 +235,10 @@
     find_slots()
     for j in range(2, nc):
         add_pair(j)
+    stat_load = pltpu.make_async_copy(stats_hbm, stat_ref, load_sem.at[0])
+    root_load = pltpu.make_async_copy(roots_hbm, root_ref, load_sem.at[1])
+    stat_load.start()
+    root_load.start()
 
     for j in range(nc):
         cols = pl.ds(*CHUNKS[j])
@@ -326,7 +326,7 @@
     square = bf((order, order))
     return pl.pallas_call(
         kernel,
-        out_shape=jax.ShapeDtypeStruct((blocks, rows, order), jnp.bfloat16),
+        out_shape=pltpu.VMEM((blocks, rows, order), jnp.bfloat16),
         in_specs=[pl.BlockSpec(memory_space=pltpu.HBM)] * 5,
         out_specs=pl.BlockSpec(memory_space=pltpu.VMEM),
         scratch_shapes=[
@@ -350,7 +350,7 @@
         + [
             bf((2, order, order)),
             dma((4,)),
-            dma((nc, chips)),
+            dma((nc,)),
             dma((nc, chips)),
             dma((nc, chips)),
             dma((nc, chips - 1)),
@@ -362,7 +362,7 @@
             pltpu.SemaphoreType.REGULAR((SIDE,)),
         ],
         compiler_params=pltpu.CompilerParams(
-            collective_id=0, has_side_effects=True, vmem_limit_bytes=53 * 2**20 + 2**19
+            collective_id=0, has_side_effects=True, vmem_limit_bytes=56 * 2**20
         ),
     )(
         partials.reshape(chips, 2, blocks, rows, order),

time: 59.8 us -> 58.3 us (0.975)
  local copies, waits for them, and re-layouts: 2.01 us -> 0.68 us
    unnamed x5 -> x1, local copies, waits for them, and re-layouts: 2.01 us -> 0.68 us
where the time goes in v4:
time: 58.3 us; the launch traced here: 58.2 us
  Pallas kernels  57.5 us (99%)
  local copies, waits for them, and re-layouts  0.68 us (1%)
    pallas_call x1, Pallas kernels, on_device(): pl.pallas_call(kernel, out_shape=pltpu.VMEM((blocks, rows, order), jnp.bf...  57.5 us

profile of v4, /device:TPU:8, one launch (start us, length us, event | category | flops | bytes accessed | tf_op | source)
XLA Modules:
  0.0 58.2 jit_solution(3884050668459151702)
XLA Ops:
  0.0 57.5 %shard_map.55 = bf16[24,8,512]{2,1,0:T(8,128)(2,1)S(1)} custom-call(bf16[4,2,24,8,512]{4,3,2,1,0:T(8,128)(2,1)} %bitcast.4, f32[2,512,512]{2,1,0:T(8,128)} %bitcast.3, bf16[2,512,512]{2,1,0:T(8,128)(2,1)} %bitcast.5, s32[192]{0:T(256)} %owner_hbm.1, s32[64]{0:T(128)} %refresh_hbm.1), custom_call_target="tpu_custom_call" | custom-call | tf_op jit(solution)/shard_map/pallas_call | solution.py:327
  57.5 0.7 %copy.7 = bf16[24,8,512]{2,1,0:T(8,128)(2,1)} copy(bf16[24,8,512]{2,1,0:T(8,128)(2,1)S(1)} %shard_map.55) | data formatting | bytes 393216

commit v5 on v4

--- a/solution.py
+++ b/solution.py
@@ -56,7 +56,7 @@
         put(rows, stat_ref[side, rows, :] * scale, m_ref, f_ref)
 
 
-def compute(take, g_ref, gt_ref, stat_ref, root_ref, m, f, x, q, t, raw_ref, dir_ref):
+def compute(take, g_ref, gt_ref, stat_ref, root_ref, m, f, x, q, t, raw_ref):
     order = g_ref.shape[0]
     normalized(stat_ref, 0, g_ref, gt_ref, m[0], f[0])
     normalized(stat_ref, 1, gt_ref, g_ref, m[1], f[1])
@@ -97,12 +97,9 @@
         raw_sq = raw_sq + jnp.sum(raw * raw, axis=0, keepdims=True)
         g32 = g_ref[rows, :].astype(jnp.float32)
         grad_sq = grad_sq + jnp.sum(g32 * g32, axis=0, keepdims=True)
-    scale = jnp.sqrt(jnp.full((1, order), jnp.sum(grad_sq), jnp.float32)) / jnp.sqrt(
+    return jnp.sqrt(jnp.full((1, order), jnp.sum(grad_sq), jnp.float32)) / jnp.sqrt(
         jnp.full((1, order), jnp.sum(raw_sq) + EPSILON, jnp.float32)
     )
-    for i in range(0, order, NB):
-        d = (stat_ref[0, pl.ds(i, NB), :] * scale).reshape(NB // 8, 8, order)
-        dir_ref[pl.ds(i // 8, NB // 8)] = d.astype(jnp.bfloat16)
 
 
 def kernel(
@@ -288,14 +285,18 @@
     stat_load.wait()
     root_load.wait()
     take = jnp.full((1, order), fresh, jnp.int32) > 0
-    compute(
+    scale = compute(
         take, g_ref, gt_ref, stat_ref, root_ref, (m0, m1), (f0, f1), (x0, x1), (q0, q1), (t0, t1),
-        raw_ref, dirs,
+        raw_ref,
     )
 
     turn = 1 - 2 * lax.rem(z + y, 2)
 
     def send_back(row):
+        high = side * rows8
+        raw = stat_ref[0, pl.ds(pl.multiple_of(row * high, high), high), :]
+        dirs[pl.ds(row * side, side)] = (raw * scale).reshape(side, rows8, order).astype(jnp.bfloat16)
+
         def one(i, carry):
             r_copy(row * side + lax.rem(y + turn * i + side, side)).start()
             return carry

time: 58.3 us -> 58.3 us (level)
  no operation moved by 1% of the time
where the time goes in v5:
time: 58.3 us; the launch traced here: 58.1 us
  Pallas kernels  57.4 us (98%)
  local copies, waits for them, and re-layouts  0.68 us (1%)
    pallas_call x1, Pallas kernels, on_device(): pl.pallas_call(kernel, out_shape=pltpu.VMEM((blocks, rows, order), jnp.bf...  57.4 us

profile of v5, /device:TPU:8, one launch (start us, length us, event | category | flops | bytes accessed | tf_op | source)
XLA Modules:
  0.0 58.1 jit_solution(17845188237024707926)
XLA Ops:
  0.0 57.4 %shard_map.55 = bf16[24,8,512]{2,1,0:T(8,128)(2,1)S(1)} custom-call(bf16[4,2,24,8,512]{4,3,2,1,0:T(8,128)(2,1)} %bitcast.4, f32[2,512,512]{2,1,0:T(8,128)} %bitcast.3, bf16[2,512,512]{2,1,0:T(8,128)(2,1)} %bitcast.5, s32[192]{0:T(256)} %owner_hbm.1, s32[64]{0:T(128)} %refresh_hbm.1), custom_call_target="tpu_custom_call" | custom-call | tf_op jit(solution)/shard_map/pallas_call | solution.py:328
  57.5 0.7 %copy.7 = bf16[24,8,512]{2,1,0:T(8,128)(2,1)} copy(bf16[24,8,512]{2,1,0:T(8,128)(2,1)S(1)} %shard_map.55) | data formatting | bytes 393216
